TPU v7x, 32 devices: a whole 2x2x4 slice. The times are simulated.
32 devices in a mesh: groups: 1, pool: 16 (over z, y, core), head: 2 (over x), sub: 1.
Axes of the slice: x: 2, y: 2, z: 4, core: 2. Of those that a mesh axis runs over, the one named last changes fastest.
Arguments:
- queries: bfloat16 [4096, 36864], P(('groups', 'pool'), ('head', 'sub')), may hold values from -64 to 64, as said below
- pool_cache: bfloat16 [64, 36864], P(('groups', 'pool')), may hold values from -5 to 5
- new_blocks: bfloat16 [64, 36864], P(('groups', 'pool')), may hold values from -5 to 5, as said below
- w_uv: bfloat16 [64, 512, 128], P(('head', 'sub')), may hold values from -0.25 to 0.25
- owners: int32 [64, 8, 1], P('groups'), may hold values from 0 to 15; in each aligned block of 32 rows (0 to 31, 32 to 63, ..., all dimensions but the last counted through in order) at most 4 rows name the same one
- slots: int32 [64, 8], P('groups'), may hold values from 0 to 3
- prefix_len: int32 [64], P('groups'), may hold values from 1 to 512, 16384 in all
- new_len: int32 [64], P('groups'), may hold values from 1 to 64, 3072 in all
- dest: int32 [64, 1], P('groups'), may hold values from 0 to 15; in each aligned block of 4 rows (0 to 3, 4 to 7, ...) no two rows name the same one
Outputs:
- attn_out: bfloat16 [4096, 8192], P(('groups', 'pool'), ('head', 'sub'))
- decode_cache: bfloat16 [256, 36864], P(('groups', 'pool'), ('head', 'sub'))
Inputs may be any that keep to these rules, and one draw needn't show every extreme that they name: `queries`: custom draw. `new_blocks`: custom draw. `owners`: the 32 list entries of the requests of one pool device name no pool device more than 4 times; some pool device's entries name some device exactly 4 times. `prefix_len`: the longest prefix is exactly 512 tokens. `new_len`: some request has exactly 64 new tokens. `dest`: the 4 requests of one pool device go to 4 different decode groups.
All inputs are finite; a program needn't handle non-finite values.
Results may differ from a plain program's by a relative error of at most 0.0051.
Values may be sent and summed in bfloat16 or wider, within the bound.
A program may use at most 128 MiB of HBM per device.

v0:
```python
import functools
import math

import jax
import jax.numpy as jnp
from jax import lax
from jax.experimental import pallas as pl
from jax.experimental.pallas import tpu as pltpu
from jax.sharding import PartitionSpec as P

KVL = 512
LAT = 576
VH = 128
BLK = 64
C = 64
MAXB = 8
POOL_DEV = 4
REQ_DEV = 4
WIN = 640
KEYS = (MAXB + 1) * BLK
TOK = 32
PACK = BLK * LAT // 128
TILES = KVL // 128

EXP_SCALE = 192.0 ** -0.5 * math.log2(math.e)
FAR_BELOW = -1e30


def attend_kernel(
    owners, slots, prefix_len, new_len,
    queries, gathered, fresh, w_uv, out,
    q_buf, key_buf, w_buf, keys_t, keys_v, rope, latent, q_sem, key_sem, fresh_sem, w_sem,
):
    heads = w_uv.shape[0]
    pairs = heads // 2
    first = lax.axis_index("pool") * REQ_DEV

    def q_copy(r):
        return pltpu.make_async_copy(
            queries.at[pl.ds(r * C, C)], q_buf.at[pl.ds(r * C, C)], q_sem.at[r]
        )

    def key_copy(r, k):
        row = owners[k, first + r] * POOL_DEV + slots[k, first + r]
        return pltpu.make_async_copy(
            gathered.at[row], key_buf.at[r, k + 1], key_sem.at[r, k]
        )

    def fresh_copy(r):
        return pltpu.make_async_copy(
            fresh.at[r], key_buf.at[r, 0], fresh_sem.at[r]
        )

    w_copy = pltpu.make_async_copy(w_uv, w_buf, w_sem)
    for r in range(REQ_DEV):
        fresh_copy(r).start()
        for k in range(MAXB):
            key_copy(r, k).start()
        q_copy(r).start()
    w_copy.start()

    keys_t[...] = jnp.zeros_like(keys_t)
    keys_v[pl.ds(KEYS, WIN - KEYS), :] = jnp.zeros((WIN - KEYS, KVL), jnp.bfloat16)

    def run(r, width, plen, nlen):
        def chunk(i, carry):
            tok = pl.multiple_of(i * TOK, TOK)
            row = pl.multiple_of(r * C + tok, TOK)
            col = lax.broadcasted_iota(jnp.int32, (TOK, width), 1)
            pos = lax.broadcasted_iota(jnp.int32, (TOK, width), 0) + tok
            last = jnp.where(col < BLK, pos, plen + BLK - 1)
            slot = col % BLK
            token = col - slot + 2 * (slot % (BLK // 2)) + slot // (BLK // 2)
            bias = jnp.where(token <= last, 0.0, FAR_BELOW)
            for parity in range(2):
                shift = parity * KVL
                q = jnp.concatenate(
                    [q_buf[pl.ds(row, TOK), pl.ds(g * 2 * LAT + shift, WIN)] for g in range(pairs)], axis=0
                )
                s = jnp.dot(q, keys_t[parity, :, :width], preferred_element_type=jnp.float32)
                s = (s.reshape(pairs, TOK, width) + bias[None]).reshape(pairs * TOK, width)
                top = jnp.max(s, axis=1, keepdims=True)
                p = jnp.exp2((s - top) * EXP_SCALE)
                total = jnp.sum(p, axis=1, keepdims=True)
                o = jnp.dot(p.astype(jnp.bfloat16), keys_v[:width], preferred_element_type=jnp.float32)
                o = (o * (1.0 / total)).astype(jnp.bfloat16)
                for g in range(pairs):
                    latent[2 * g + parity, pl.ds(row, TOK), :] = o[g * TOK:(g + 1) * TOK]
            return carry

        lax.fori_loop(0, (nlen + TOK - 1) // TOK, chunk, 0)

    def request(r, carry):
        plen = prefix_len[first + r]
        nlen = new_len[first + r]
        fresh_copy(r).wait()
        for k in range(MAXB):
            key_copy(r, k).wait()
        for k in range(MAXB + 1):
            for j in range(TILES):
                keys_v[pl.ds(k * BLK, BLK), pl.ds(j * 128, 128)] = key_buf[r, k, pl.ds(j * BLK, BLK), :]
            tail = key_buf[r, k, pl.ds(TILES * BLK, BLK // 2), :]
            rope[pl.ds(k * BLK, BLK // 2), :] = tail[:, :LAT - KVL]
            rope[pl.ds(k * BLK + BLK // 2, BLK // 2), :] = tail[:, LAT - KVL:]
        flipped = keys_v[pl.ds(0, KEYS), :].T
        keys_t[0, pl.ds(0, KVL), pl.ds(0, KEYS)] = flipped
        keys_t[1, pl.ds(WIN - LAT, KVL), pl.ds(0, KEYS)] = flipped
        flipped = rope[...].T
        keys_t[0, pl.ds(KVL, LAT - KVL), pl.ds(0, KEYS)] = flipped
        keys_t[1, pl.ds(WIN - LAT + KVL, LAT - KVL), pl.ds(0, KEYS)] = flipped
        q_copy(r).wait()
        pl.when(plen <= 192)(lambda: run(r, 256, plen, nlen))
        pl.when((plen > 192) & (plen <= 448))(lambda: run(r, 512, plen, nlen))
        pl.when(plen > 448)(lambda: run(r, WIN, plen, nlen))
        return carry

    lax.fori_loop(0, REQ_DEV, request, 0)
    w_copy.wait()

    rows = REQ_DEV * C
    at = lax.broadcasted_iota(jnp.int32, (rows, VH), 0)
    live = jnp.zeros((rows, VH), jnp.int32)
    for r in range(REQ_DEV):
        live = jnp.where((at >= r * C) & (at < r * C + new_len[first + r]), 1, live)

    def project(h, carry):
        value = jnp.dot(latent[h], w_buf[h], preferred_element_type=jnp.float32)
        out[:, pl.ds(pl.multiple_of(h * VH, VH), VH)] = jnp.where(live == 1, value, 0.0).astype(out.dtype)
        return carry

    lax.fori_loop(0, heads, project, 0, unroll=4)


def attend(queries, gathered, fresh, w_uv, owners, slots, prefix_len, new_len):
    heads = w_uv.shape[0]
    rows = REQ_DEV * C
    flops = 2 * rows * heads * (KEYS * (LAT + KVL) + KVL * VH)
    return pl.pallas_call(
        attend_kernel,
        grid_spec=pltpu.PrefetchScalarGridSpec(
            num_scalar_prefetch=4,
            grid=(1,),
            in_specs=[pl.BlockSpec(memory_space=pl.ANY)] * 4,
            out_specs=pl.BlockSpec((rows, heads * VH), lambda i, *_: (0, 0)),
            scratch_shapes=[
                pltpu.VMEM((rows, heads * LAT), jnp.bfloat16),
                pltpu.VMEM((REQ_DEV, MAXB + 1, PACK, 128), jnp.bfloat16),
                pltpu.VMEM(w_uv.shape, jnp.bfloat16),
                pltpu.VMEM((2, WIN, WIN), jnp.bfloat16),
                pltpu.VMEM((WIN, KVL), jnp.bfloat16),
                pltpu.VMEM((KEYS, LAT - KVL), jnp.bfloat16),
                pltpu.VMEM((heads, rows, KVL), jnp.bfloat16),
                pltpu.SemaphoreType.DMA((REQ_DEV,)),
                pltpu.SemaphoreType.DMA((REQ_DEV, MAXB)),
                pltpu.SemaphoreType.DMA((REQ_DEV,)),
                pltpu.SemaphoreType.DMA,
            ],
        ),
        out_shape=jax.ShapeDtypeStruct((rows, heads * VH), jnp.bfloat16),
        compiler_params=pltpu.CompilerParams(vmem_limit_bytes=56 * 1024 * 1024),
        cost_estimate=pl.CostEstimate(flops=flops, bytes_accessed=queries.size * 2, transcendentals=rows * heads * KEYS),
        name="attend",
    )(owners, slots, prefix_len, new_len, queries, gathered, fresh, w_uv)


def gather_kernel(
    goes, lens, pool, fresh, out, leaving, fresh_out, packed, raw, own_sem,
    z_send, z_recv, y_send, y_recv, x_send, x_recv, far_send, far_recv, c_send, c_recv,
):
    me = lax.axis_index("pool")
    x = lax.axis_index("head")
    z, y, c = me // 4, (me // 2) % 2, me % 2
    lane = lax.broadcasted_iota(jnp.int32, (BLK // 2, 128), 1)

    def spread(ref):
        def step(i, carry):
            at = pl.multiple_of(i * 256, 256)
            both = jnp.concatenate([ref[:, pl.ds(at, 128)], ref[:, pl.ds(at + 128, 128)]], axis=0)
            raw[pl.ds(pl.multiple_of(i * 8, 8), 8), :] = both.astype(jnp.float32)
            return carry

        lax.fori_loop(0, PACK // 2, step, 0, unroll=8)

    def pack(ref):
        for b in range(POOL_DEV):
            nine = [raw[pl.ds(POOL_DEV * j + b, BLK // 2, stride=9 * POOL_DEV), :] for j in range(9)]
            turned = [pltpu.roll(row, 64, 1) for row in nine[4:]]
            for j in range(TILES):
                odd = jnp.where(lane < 64, turned[j], turned[j + 1])
                ref[b, pl.ds(j * BLK, BLK), :] = jnp.concatenate([nine[j], odd], axis=0).astype(ref.dtype)
            ref[b, pl.ds(TILES * BLK, BLK // 2), :] = jnp.where(lane < 64, nine[4], nine[8]).astype(ref.dtype)

    def group(zz, yy, cc):
        return zz * 4 + yy * 2 + cc

    below, above = {"pool": me - 4}, {"pool": me + 4}
    beside, across, sibling = {"pool": group(z, 1 - y, c)}, {"head": 1 - x}, {"pool": group(z, y, 1 - c)}

    barrier = pltpu.get_barrier_semaphore()

    def greet(device):
        pl.semaphore_signal(barrier, inc=1, device_id=device, device_id_type=pl.DeviceIdType.MESH)

    for device in (beside, across, sibling):
        greet(device)
    pl.when(z > 0)(lambda: greet(below))
    pl.when(z < 3)(lambda: greet(above))

    spread(pool)
    pack(packed)

    inner = (z > 0) & (z < 3)
    end = jnp.logical_not(inner)
    pl.when(inner)(lambda: pl.semaphore_wait(barrier, 5))
    pl.when(end)(lambda: pl.semaphore_wait(barrier, 4))

    def real(l):
        return l + x * (3 - 2 * l)

    def copy(g, l, send, recv, device, own=False):
        src = packed.at[real(l)] if own else out.at[g, real(l)]
        return pltpu.make_async_remote_copy(
            src_ref=src, dst_ref=out.at[g, real(l)], send_sem=send, recv_sem=recv,
            device_id=device, device_id_type=pl.DeviceIdType.MESH,
        )

    def z_copy(zz, l, up, own=False):
        return copy(group(zz, y, c), l, z_send.at[up, zz, l], z_recv.at[zz, l], above if up else below, own)

    def y_copy(zz, yy, l, own=False):
        return copy(group(zz, yy, c), l, y_send.at[zz, l], y_recv.at[zz, l], beside, own)

    def x_copy(zz, l, came=False):
        return copy(group(zz, 1 - y, c), 3 - l if came else l, x_send.at[zz, l], x_recv.at[zz, l], across)

    def far_copy(l, came=False):
        return copy(group(3 - z, y, c), 3 - l if came else l, far_send.at[l], far_recv.at[l], across)

    def c_copy(zz, yy, cc, l, own=False):
        return copy(group(zz, yy, cc), l, c_send.at[zz, yy, l], c_recv.at[zz, yy, l], sibling, own)

    def each(distance, act):
        if distance == 0:
            act(z, None)
        else:
            pl.when(z + distance <= 3)(lambda: act(z + distance, False))
            pl.when(z - distance >= 0)(lambda: act(z - distance, True))

    def z_round(distance):
        own = distance == 0
        for l in range(2 if distance == 3 else 4):
            def line(zz, up, l=l):
                if not own:
                    z_copy(zz, l, up).wait_recv()
                if distance < 2 or l < 2:
                    if up is None or up:
                        pl.when(z < 3)(lambda: z_copy(zz, l, 1, own).start())
                    if up is None or not up:
                        pl.when(z > 0)(lambda: z_copy(zz, l, 0, own).start())
                if l < 2:
                    y_copy(zz, y, l, own).start()
                if distance == 3:
                    far_copy(l).start()
                c_copy(zz, y, c, l, own).start()

            each(distance, line)

    def y_round(distance):
        for l in range(2):
            def side(zz, up, l=l):
                y_copy(zz, 1 - y, l).wait_recv()
                x_copy(zz, l).start()
                c_copy(zz, 1 - y, c, l).start()

            each(distance, side)

    def x_round(distance):
        for l in range(2):
            def side(zz, up, l=l):
                x_copy(zz, l, True).wait_recv()
                c_copy(zz, 1 - y, c, 3 - l).start()

            each(distance, side)

    z_round(0)
    own_copy = pltpu.make_async_copy(packed, out.at[me], own_sem)
    own_copy.start()

    z_round(1)
    y_round(0)

    spread(fresh)
    pack(fresh_out)
    span = leaving.shape[1]
    start = x * span
    place = (lax.broadcasted_iota(jnp.int32, (span, 128), 0) + start) * 128 + lax.broadcasted_iota(jnp.int32, (span, 128), 1)
    rows = []
    for r in range(REQ_DEV):
        value = raw[pl.ds(start * REQ_DEV + r, span, stride=REQ_DEV), :]
        target = jnp.full((span, 128), goes[me * REQ_DEV + r], jnp.int32)
        rows.append((target, jnp.where(place < lens[me * REQ_DEV + r] * LAT, value, 0.0)))
    for n in range(leaving.shape[0]):
        row = jnp.zeros((span, 128), jnp.float32)
        for target, value in rows:
            row = jnp.where(target == n, value, row)
        leaving[n] = row.astype(leaving.dtype)

    z_round(2)
    x_round(0)
    y_round(1)
    z_round(3)
    x_round(1)
    y_round(2)
    x_round(2)
    y_round(3)

    def far_round():
        for l in range(2):
            far_copy(l, True).wait_recv()
            c_copy(3 - z, y, c, 3 - l).start()

    pl.when(end)(far_round)
    x_round(3)

    own_copy.wait()
    for zz in range(4):
        for yy in range(2):
            for l in range(4):
                c_copy(zz, yy, 1 - c, l).wait_recv()

    for zz in range(4):
        for l in range(4):
            reach = 3 if l < 2 else 1
            pl.when((z < 3) & (zz <= z) & (z - zz <= reach))(lambda zz=zz, l=l: z_copy(zz, l, 1).wait_send())
            pl.when((z > 0) & (zz >= z) & (zz - z <= reach))(lambda zz=zz, l=l: z_copy(zz, l, 0).wait_send())
            for yy in range(2):
                c_copy(zz, yy, c, l).wait_send()
        for l in range(2):
            y_copy(zz, y, l).wait_send()
            x_copy(zz, l).wait_send()

    def far_sent():
        for l in range(2):
            far_copy(l).wait_send()

    pl.when(end)(far_sent)


def gather_pool(pool_cache, new_blocks, dest, new_len):
    pool_count = lax.axis_size("pool")
    span = PACK // lax.axis_size("head")
    dma = pltpu.SemaphoreType.DMA
    kind = pool_cache.dtype
    vmem, smem = pl.BlockSpec(memory_space=pltpu.VMEM), pl.BlockSpec(memory_space=pltpu.SMEM)
    return pl.pallas_call(
        gather_kernel,
        out_shape=(
            jax.ShapeDtypeStruct((pool_count, POOL_DEV, PACK, 128), kind),
            jax.ShapeDtypeStruct((pool_count, span, 128), kind),
            jax.ShapeDtypeStruct((REQ_DEV, PACK, 128), kind),
        ),
        in_specs=[smem, smem, vmem, vmem],
        out_specs=(pl.BlockSpec(memory_space=pl.ANY), vmem, vmem),
        scratch_shapes=[
            pltpu.VMEM((POOL_DEV, PACK, 128), kind), pltpu.VMEM((POOL_DEV * PACK, 128), jnp.float32), dma,
            dma((2, 4, 4)), dma((4, 4)), dma((4, 2)), dma((4, 2)), dma((4, 2)), dma((4, 2)), dma((2,)), dma((2,)),
            dma((4, 2, 4)), dma((4, 2, 4)),
        ],
        compiler_params=pltpu.CompilerParams(
            collective_id=0, has_side_effects=True, vmem_limit_bytes=56 * 1024 * 1024
        ),
        name="gather_pool",
    )(dest, new_len, pool_cache, new_blocks)


def pack_blocks(blocks):
    blocks = blocks.reshape(-1, BLK // 2, 2, LAT).transpose(0, 2, 1, 3).reshape(-1, BLK, LAT)
    lanes = blocks[:, :, :KVL].reshape(-1, BLK, TILES, 128).transpose(0, 2, 1, 3).reshape(-1, TILES * BLK, 128)
    tail = jnp.concatenate([blocks[:, :BLK // 2, KVL:], blocks[:, BLK // 2:, KVL:]], axis=2)
    return jnp.concatenate([lanes, tail], axis=1)


def decode_rows(new_blocks, new_len, dest, own):
    pool_count = lax.axis_size("pool")
    share = new_blocks.shape[1] // lax.axis_size(("head", "sub"))
    start = lax.axis_index(("head", "sub")) * share
    part = lax.dynamic_slice_in_dim(new_blocks, start, share, 1)
    tok = (jnp.arange(share, dtype=jnp.int32) + start) // LAT
    lens = lax.dynamic_slice_in_dim(new_len, own, REQ_DEV, 0)
    goes = lax.dynamic_slice_in_dim(dest[:, 0], own, REQ_DEV, 0)
    part = jnp.where(tok[None, :] < lens[:, None], part, 0)
    rows = jnp.zeros((pool_count, share), new_blocks.dtype)
    for r in range(REQ_DEV):
        rows = jnp.where((goes[r] == jnp.arange(pool_count))[:, None], part[r][None, :], rows)
    return rows.reshape(pool_count, share // 128, 128)


def body(queries, pool_cache, new_blocks, w_uv, owners, slots, prefix_len, new_len, dest):
    own = lax.axis_index("pool") * REQ_DEV
    sizes = tuple(lax.axis_size(name) for name in ("groups", "pool", "head", "sub"))
    if sizes == (1, 16, 2, 1):
        gathered, leaving, fresh = gather_pool(pool_cache, new_blocks, dest[:, 0], new_len)
        gathered = gathered.reshape(-1, PACK, 128)
    else:
        gathered = lax.all_gather(pack_blocks(pool_cache), "pool", axis=0, tiled=True)
        fresh = pack_blocks(new_blocks)
        leaving = decode_rows(new_blocks, new_len, dest, own)
        gathered, leaving = lax.optimization_barrier((gathered, leaving))
    arrived = lax.all_to_all(leaving, "pool", split_axis=0, concat_axis=0, tiled=True)
    attn_out = attend(queries, gathered, fresh, w_uv, owners[:, :, 0].T, slots.T, prefix_len, new_len)
    decode_cache = arrived.reshape(arrived.shape[0], -1)
    return attn_out, decode_cache


def solution(mesh):
    placed = (
        P(("groups", "pool"), ("head", "sub")),
        P(("groups", "pool"), None),
        P(("groups", "pool"), None),
        P(("head", "sub"), None, None),
        P("groups", None, None),
        P("groups", None),
        P("groups"),
        P("groups"),
        P("groups", None),
    )
    return jax.shard_map(
        body,
        mesh=mesh,
        in_specs=placed,
        out_specs=(P(("groups", "pool"), ("head", "sub")), P(("groups", "pool"), ("head", "sub"))),
        check_vma=False,
    )
```

profile of v0, /device:TPU:9, one launch (start us, length us, event | category | flops | bytes accessed | tf_op | source)
XLA Modules:
  0.0 70.0 jit_solution(18093999162422696791)
XLA Ops:
  0.6 33.5 %gather_pool.1 = (bf16[16,4,288,128]{3,2,1,0:T(8,128)(2,1)}, bf16[16,144,128]{2,1,0:T(8,128)(2,1)}, bf16[4,288,128]{2,1,0:T(8,128)(2,1)}) custom-call(s32[64]{0:T(128)} %bitcast.12, s32[64]{0:T(128)} %new_len.1, bf16[4,36864]{1,0:T(4,128)(2,1)} %pool.1, bf16[4,36864]{1,0:T(4,128)(2,1)} %fresh.1), custom_call_target="tpu_custom_call" | custom-call | tf_op jit(solution)/shard_map/gather_pool/pallas_call | solution.py:355
  34.2 9.3 %all-to-all-start = ((bf16[16,144,128]{2,1,0:T(8,128)(2,1)}), bf16[16,144,128]{2,1,0:T(8,128)(2,1)S(1)}, u32[]{:S(2)}, u32[]{:S(2)}) async-start(bf16[16,144,128]{2,1,0:T(8,128)(2,1)} %get-tuple-element.7), calls=%async_computation | async-start | bytes 1179648 | tf_op jit(solution)/shard_map/all_to_all | solution.py:409
  43.5 25.6 %attend.1 = bf16[256,4096]{1,0:T(8,128)(2,1)} custom-call(s32[8,64]{1,0:T(8,128)} %bitcast.14, s32[8,64]{1,0:T(8,128)} %bitcast.15, s32[64]{0:T(128)} %prefix_len.1, s32[64]{0:T(128)} %new_len.1, bf16[256,18432]{1,0:T(8,128)(2,1)} %queries.1, bf16[64,288,128]{2,1,0:T(8,128)(2,1)} %bitcast.13, bf16[4,288,128]{2,1,0:T(8,128)(2,1)} %get-tuple-element.6.fresh, ...), custom_call_target="tpu_custom_call" | custom-call | flops 11341398016 | bytes 9437184 | tf_op jit(solution)/shard_map/attend/pallas_call | solution.py:138
  69.0 0.0 all-to-all-done
  69.1 1.0 %copy.13 = bf16[2,8,144,128]{3,1,2,0:T(8,128)(2,1)} copy(bf16[2,8,144,128]{3,2,1,0:T(8,128)(2,1)S(1)} %bitcast.10) | data formatting | bytes 1179648
Async XLA Ops:
  34.2 34.9 %all-to-all-start = ((bf16[16,144,128]{2,1,0:T(8,128)(2,1)}), bf16[16,144,128]{2,1,0:T(8,128)(2,1)S(1)}, u32[]{:S(2)}, u32[]{:S(2)}) async-start(bf16[16,144,128]{2,1,0:T(8,128)(2,1)} %get-tuple-element.7), calls=%async_computation | async-start | bytes 1179648 | tf_op jit(solution)/shard_map/all_to_all | solution.py:409
where the time goes:
time: 70.9 us; the launch traced here: 70 us
  Pallas kernels  59.1 us (83%)
  starting transfers between devices  9.31 us (13%)
  local copies, waits for them, and re-layouts  0.97 us (1%)
    pallas_call x1, Pallas kernels, gather_pool(): pl.pallas_call(gather_kernel, out_shape=(jax.ShapeDtypeStruct((pool_count...  33.5 us
    pallas_call x1, Pallas kernels, attend(): pl.pallas_call(attend_kernel, grid_spec=pltpu.PrefetchScalarGridSpec(num_...  25.6 us
    all_to_all x1, starting transfers between devices, body(): lax.all_to_all(leaving, 'pool', split_axis=0, concat_axis=0, tiled=True)  9.31 us
  transfers between devices with their start and end apart: 1, of which 0 were waited for; matrix products, arithmetic and copies ran while one was open for 0% of the time, Pallas kernels for 37%

commit v1 on v0

--- a/solution.py
+++ b/solution.py
@@ -62,7 +62,24 @@
     keys_t[...] = jnp.zeros_like(keys_t)
     keys_v[pl.ds(KEYS, WIN - KEYS), :] = jnp.zeros((WIN - KEYS, KVL), jnp.bfloat16)
 
+    def build(r, width):
+        count = min(width, KEYS)
+        for k in range(count // BLK):
+            for j in range(TILES):
+                keys_v[pl.ds(k * BLK, BLK), pl.ds(j * 128, 128)] = key_buf[r, k, pl.ds(j * BLK, BLK), :]
+            tail = key_buf[r, k, pl.ds(TILES * BLK, BLK // 2), :]
+            rope[pl.ds(k * BLK, BLK // 2), :] = tail[:, :LAT - KVL]
+            rope[pl.ds(k * BLK + BLK // 2, BLK // 2), :] = tail[:, LAT - KVL:]
+        flipped = keys_v[pl.ds(0, count), :].T
+        keys_t[0, pl.ds(0, KVL), pl.ds(0, count)] = flipped
+        keys_t[1, pl.ds(WIN - LAT, KVL), pl.ds(0, count)] = flipped
+        flipped = rope[pl.ds(0, count), :].T
+        keys_t[0, pl.ds(KVL, LAT - KVL), pl.ds(0, count)] = flipped
+        keys_t[1, pl.ds(WIN - LAT + KVL, LAT - KVL), pl.ds(0, count)] = flipped
+
     def run(r, width, plen, nlen):
+        build(r, width)
+
         def chunk(i, carry):
             tok = pl.multiple_of(i * TOK, TOK)
             row = pl.multiple_of(r * C + tok, TOK)
@@ -96,18 +113,6 @@
         fresh_copy(r).wait()
         for k in range(MAXB):
             key_copy(r, k).wait()
-        for k in range(MAXB + 1):
-            for j in range(TILES):
-                keys_v[pl.ds(k * BLK, BLK), pl.ds(j * 128, 128)] = key_buf[r, k, pl.ds(j * BLK, BLK), :]
-            tail = key_buf[r, k, pl.ds(TILES * BLK, BLK // 2), :]
-            rope[pl.ds(k * BLK, BLK // 2), :] = tail[:, :LAT - KVL]
-            rope[pl.ds(k * BLK + BLK // 2, BLK // 2), :] = tail[:, LAT - KVL:]
-        flipped = keys_v[pl.ds(0, KEYS), :].T
-        keys_t[0, pl.ds(0, KVL), pl.ds(0, KEYS)] = flipped
-        keys_t[1, pl.ds(WIN - LAT, KVL), pl.ds(0, KEYS)] = flipped
-        flipped = rope[...].T
-        keys_t[0, pl.ds(KVL, LAT - KVL), pl.ds(0, KEYS)] = flipped
-        keys_t[1, pl.ds(WIN - LAT + KVL, LAT - KVL), pl.ds(0, KEYS)] = flipped
         q_copy(r).wait()
         pl.when(plen <= 192)(lambda: run(r, 256, plen, nlen))
         pl.when((plen > 192) & (plen <= 448))(lambda: run(r, 512, plen, nlen))
@@ -164,7 +169,7 @@
 
 
 def gather_kernel(
-    goes, lens, pool, fresh, out, leaving, fresh_out, packed, raw, own_sem,
+    goes, lens, pool, fresh, out, decode, fresh_out, packed, raw, leaving, own_sem, stay_sem, push_send, push_recv,
     z_send, z_recv, y_send, y_recv, x_send, x_recv, far_send, far_recv, c_send, c_recv,
 ):
     me = lax.axis_index("pool")
@@ -201,18 +206,17 @@
     def greet(device):
         pl.semaphore_signal(barrier, inc=1, device_id=device, device_id_type=pl.DeviceIdType.MESH)
 
-    for device in (beside, across, sibling):
-        greet(device)
-    pl.when(z > 0)(lambda: greet(below))
-    pl.when(z < 3)(lambda: greet(above))
+    peers = decode.shape[0]
+    greet(across)
+    for n in range(1, peers):
+        greet({"pool": (me + n) % peers})
 
     spread(pool)
     pack(packed)
 
     inner = (z > 0) & (z < 3)
     end = jnp.logical_not(inner)
-    pl.when(inner)(lambda: pl.semaphore_wait(barrier, 5))
-    pl.when(end)(lambda: pl.semaphore_wait(barrier, 4))
+    pl.semaphore_wait(barrier, peers)
 
     def real(l):
         return l + x * (3 - 2 * l)
@@ -286,9 +290,6 @@
     own_copy = pltpu.make_async_copy(packed, out.at[me], own_sem)
     own_copy.start()
 
-    z_round(1)
-    y_round(0)
-
     spread(fresh)
     pack(fresh_out)
     span = leaving.shape[1]
@@ -305,7 +306,28 @@
             row = jnp.where(target == n, value, row)
         leaving[n] = row.astype(leaving.dtype)
 
+    def push(n):
+        peer = (me + n) % peers
+        return pltpu.make_async_remote_copy(
+            src_ref=leaving.at[peer], dst_ref=decode.at[me], send_sem=push_send.at[peer], recv_sem=push_recv.at[me],
+            device_id={"pool": peer}, device_id_type=pl.DeviceIdType.MESH,
+        )
+
+    def pushed(n):
+        peer = (me + n) % peers
+        return pltpu.make_async_remote_copy(
+            src_ref=leaving.at[peer], dst_ref=decode.at[peer], send_sem=push_send.at[peer], recv_sem=push_recv.at[peer],
+            device_id={"pool": peer}, device_id_type=pl.DeviceIdType.MESH,
+        )
+
+    stay = pltpu.make_async_copy(leaving.at[me], decode.at[me], stay_sem)
+    stay.start()
+
+    z_round(1)
+    y_round(0)
     z_round(2)
+    for n in range(1, peers):
+        push(n).start()
     x_round(0)
     y_round(1)
     z_round(3)
@@ -323,6 +345,10 @@
     x_round(3)
 
     own_copy.wait()
+    stay.wait()
+    for n in range(1, peers):
+        pushed(n).wait_recv()
+        push(n).wait_send()
     for zz in range(4):
         for yy in range(2):
             for l in range(4):
@@ -360,9 +386,10 @@
             jax.ShapeDtypeStruct((REQ_DEV, PACK, 128), kind),
         ),
         in_specs=[smem, smem, vmem, vmem],
-        out_specs=(pl.BlockSpec(memory_space=pl.ANY), vmem, vmem),
+        out_specs=(pl.BlockSpec(memory_space=pl.ANY), pl.BlockSpec(memory_space=pl.ANY), vmem),
         scratch_shapes=[
-            pltpu.VMEM((POOL_DEV, PACK, 128), kind), pltpu.VMEM((POOL_DEV * PACK, 128), jnp.float32), dma,
+            pltpu.VMEM((POOL_DEV, PACK, 128), kind), pltpu.VMEM((POOL_DEV * PACK, 128), jnp.float32),
+            pltpu.VMEM((pool_count, span, 128), kind), dma, dma, dma((pool_count,)), dma((pool_count,)),
             dma((2, 4, 4)), dma((4, 4)), dma((4, 2)), dma((4, 2)), dma((4, 2)), dma((4, 2)), dma((2,)), dma((2,)),
             dma((4, 2, 4)), dma((4, 2, 4)),
         ],
@@ -399,14 +426,14 @@
     own = lax.axis_index("pool") * REQ_DEV
     sizes = tuple(lax.axis_size(name) for name in ("groups", "pool", "head", "sub"))
     if sizes == (1, 16, 2, 1):
-        gathered, leaving, fresh = gather_pool(pool_cache, new_blocks, dest[:, 0], new_len)
+        gathered, arrived, fresh = gather_pool(pool_cache, new_blocks, dest[:, 0], new_len)
         gathered = gathered.reshape(-1, PACK, 128)
     else:
         gathered = lax.all_gather(pack_blocks(pool_cache), "pool", axis=0, tiled=True)
         fresh = pack_blocks(new_blocks)
         leaving = decode_rows(new_blocks, new_len, dest, own)
         gathered, leaving = lax.optimization_barrier((gathered, leaving))
-    arrived = lax.all_to_all(leaving, "pool", split_axis=0, concat_axis=0, tiled=True)
+        arrived = lax.all_to_all(leaving, "pool", split_axis=0, concat_axis=0, tiled=True)
     attn_out = attend(queries, gathered, fresh, w_uv, owners[:, :, 0].T, slots.T, prefix_len, new_len)
     decode_cache = arrived.reshape(arrived.shape[0], -1)
     return attn_out, decode_cache

time: 70.9 us -> 70.9 us (level)
  the two profiles are of different devices: /device:TPU:9 before, /device:TPU:0 now
where the time goes in v1:
time: 70.9 us; the launch traced here: 70.3 us
  Pallas kernels  68.7 us (97%)
  local copies, waits for them, and re-layouts  0.97 us (1%)
    pallas_call x1, Pallas kernels, gather_pool(): pl.pallas_call(gather_kernel, out_shape=(jax.ShapeDtypeStruct((pool_count...  41.7 us
    pallas_call x1, Pallas kernels, attend(): pl.pallas_call(attend_kernel, grid_spec=pltpu.PrefetchScalarGridSpec(num_...  27 us

profile of v1, /device:TPU:0, one launch (start us, length us, event | category | flops | bytes accessed | tf_op | source)
XLA Modules:
  0.0 70.3 jit_solution(7999639124084304361)
XLA Ops:
  0.6 41.7 %gather_pool.1 = (bf16[16,4,288,128]{3,2,1,0:T(8,128)(2,1)}, bf16[16,144,128]{2,1,0:T(8,128)(2,1)}, bf16[4,288,128]{2,1,0:T(8,128)(2,1)}) custom-call(s32[64]{0:T(128)} %bitcast.12, s32[64]{0:T(128)} %new_len.1, bf16[4,36864]{1,0:T(4,128)(2,1)} %pool.1, bf16[4,36864]{1,0:T(4,128)(2,1)} %fresh.1), custom_call_target="tpu_custom_call" | custom-call | tf_op jit(solution)/shard_map/gather_pool/pallas_call | solution.py:381
  42.4 0.0 copy-start
  42.4 27.0 %attend.1 = bf16[256,4096]{1,0:T(8,128)(2,1)} custom-call(s32[8,64]{1,0:T(8,128)} %bitcast.14, s32[8,64]{1,0:T(8,128)} %bitcast.15, s32[64]{0:T(128)} %prefix_len.1, s32[64]{0:T(128)} %new_len.1, bf16[256,18432]{1,0:T(8,128)(2,1)} %queries.1, bf16[64,288,128]{2,1,0:T(8,128)(2,1)} %bitcast.13, bf16[4,288,128]{2,1,0:T(8,128)(2,1)} %get-tuple-element.6.fresh, ...), custom_call_target="tpu_custom_call" | custom-call | flops 11341398016 | bytes 9437184 | tf_op jit(solution)/shard_map/attend/pallas_call | solution.py:143
  69.4 0.0 copy-done
  69.4 1.0 %copy.13 = bf16[2,8,144,128]{3,1,2,0:T(8,128)(2,1)} copy(bf16[2,8,144,128]{3,2,1,0:T(8,128)(2,1)S(1)} %bitcast.11) | data formatting | bytes 1179648
Async XLA Ops:
  42.4 27.0 %copy-start = (bf16[16,144,128]{2,1,0:T(8,128)(2,1)S(1)}, bf16[16,144,128]{2,1,0:T(8,128)(2,1)}, u32[]{:S(2)}) copy-start(bf16[16,144,128]{2,1,0:T(8,128)(2,1)} %get-tuple-element.7) | copy-start | bytes 1769476
